TPU v7x, 32 devices: a whole 2x2x4 slice. The times are simulated.
32 devices in a mesh: groups: 2 (over x), vel: 8 (over z, y), sub: 2 (over core).
Axes of the slice: x: 2, y: 2, z: 4, core: 2. Of those that a mesh axis runs over, the one named last changes fastest.
Arguments:
- dist: float32 [16, 256, 1024], P('sub', 'vel', 'groups'), parts along dimension 2, may hold values from 0 to 6, as said below
- cell_type: int32 [1024], P('groups'), parts along dimension 0, may hold values from 0 to 1, as said below
- groove_mask: int32 [64], P('groups'), parts along dimension 0, may hold values 0 or 1
Outputs:
- dist_next: float32 [16, 256, 1024], P('sub', 'vel', 'groups'), parts along dimension 2
There are 2 independent parts, one for each index of `groups`. A program takes and returns all parts, laid end to end along the dimension named above; each array names one. Nothing has to cross between parts.
Inputs may be any that keep to these rules, and one draw needn't show every extreme that they name: `cell_type`: in each column the solid cells are its lowest ones; a column holds at most a quarter of 16 of them, and every draw has columns with that many and columns with none; grooves repeat along the columns with a period of 4 to 12 columns. `dist`: every entry is positive.
All inputs are finite; a program needn't handle non-finite values.
Results may differ from a plain program's by a relative error of at most 0.0001.
Values sent between devices are 32-bit elements; how exact they have to be, the bound alone decides.
A program may use at most 128 MiB of HBM per device.

v0:
```python
import math
import jax
import jax.numpy as jnp
from jax import lax
from jax.sharding import PartitionSpec as P

VN = 16
SY = 16
STEPS = 2
VEL_RANGE = 5.0
TOP_SPEED = 1.0
ACC_LAND = 0.4
ACC_TOP = 0.7
KNUDSEN = 1.0
HIGHEST = lax.Precision.HIGHEST
FORMS = ("kj,jxzc->kxzc", "kj,yjzc->ykzc", "kj,yxjc->yxkc")


def swapped(value, axis, distance):
    mask = 2**distance
    pairs = [(source, source ^ mask) for source in range(lax.axis_size(axis))]
    return lax.ppermute(value, axis, pairs)


def spacing_of(count):
    return 2.0 * VEL_RANGE / count


def time_step(count):
    return 0.8 / ((count - 1) * spacing_of(count))


def speeds(index, count):
    return (index.astype(jnp.float32) - (count - 1) / 2.0) * spacing_of(count)


def wave_numbers(count):
    index = jnp.arange(count, dtype=jnp.int32)
    wrapped = jnp.where(index < count // 2, index, index - count)
    return wrapped.astype(jnp.float32) * (math.pi / VEL_RANGE)


def kernels(count):
    wave = wave_numbers(count)
    wave_y = wave[:, None, None]
    wave_x = wave[None, :, None]
    wave_z = wave[None, None, :]
    square = wave_y * wave_y + wave_x * wave_x + wave_z * wave_z
    first = 1.0 / (1.0 + square / 12.0)
    second = 3.0 * jnp.cos(0.9 * wave_x) / (1.0 + square / 10.0)
    damped = 1.0 + square / 9.0
    loss = 3.0 / (damped * damped)
    return (first, second, loss)


def dft_tables(count):
    index = jnp.arange(count, dtype=jnp.float32)
    angle = 2.0 * math.pi / count * index[:, None] * index[None, :]
    return (jnp.cos(angle), jnp.sin(angle))


def full_grid(count):
    index = jnp.arange(count * count * count, dtype=jnp.int32)
    velocity_y = speeds(index // (count * count), count)
    velocity_x = speeds(index // count % count, count)
    velocity_z = speeds(index % count, count)
    return (velocity_x, velocity_y, velocity_z)


def wall_tables(velocity_x, velocity_y, velocity_z):
    rest = jnp.exp(
        -(velocity_x * velocity_x + velocity_y * velocity_y + velocity_z * velocity_z) / 2.0
    )
    shifted = velocity_x - TOP_SPEED
    moving = jnp.exp(-(shifted * shifted + velocity_y * velocity_y + velocity_z * velocity_z) / 2.0)
    weights = jnp.stack(
        [
            jnp.maximum(-velocity_x, 0.0),
            jnp.maximum(velocity_x, 0.0),
            jnp.maximum(-velocity_y, 0.0),
            jnp.maximum(velocity_y, 0.0),
        ]
    )
    return (rest, moving, weights)


def wall_norms(count):
    velocity_x, velocity_y, velocity_z = full_grid(count)
    rest, moving, weights = wall_tables(velocity_x, velocity_y, velocity_z)
    return (
        jnp.sum(jnp.maximum(velocity_x, 0.0) * rest),
        jnp.sum(jnp.maximum(-velocity_x, 0.0) * rest),
        jnp.sum(jnp.maximum(velocity_y, 0.0) * rest),
        jnp.sum(jnp.maximum(-velocity_y, 0.0) * moving),
    )


def cell_masks(cell_type, groove_mask, height_count):
    total = cell_type.shape[0]
    solid = cell_type.astype(jnp.float32)
    height = jnp.arange(total, dtype=jnp.int32) % height_count
    left_solid = jnp.roll(solid, height_count)
    right_solid = jnp.roll(solid, -height_count)
    below_solid = jnp.where(height == 0, 1.0, jnp.roll(solid, 1))
    top_wall = jnp.where(height == height_count - 1, 1.0, 0.0 * solid)
    accommodation = jnp.repeat(jnp.where(groove_mask == 1, 1.0, ACC_LAND), height_count)
    return jnp.stack([left_solid, right_solid, below_solid, top_wall, accommodation, 1.0 - solid])


def advance(center, left, right, below, above, mirror, flux, masks, velocity, norms, step_size):
    velocity_x, velocity_y, rest, moving = velocity
    left_solid = masks[0][None, :]
    right_solid = masks[1][None, :]
    below_solid = masks[2][None, :]
    top_wall = masks[3][None, :]
    accommodation = masks[4][None, :]
    fluid = masks[5][None, :]
    left_ghost = (flux[0] / norms[0])[None, :] * rest
    right_ghost = (flux[1] / norms[1])[None, :] * rest
    below_ghost = (1.0 - accommodation) * mirror + accommodation * (flux[2] / norms[2])[
        None, :
    ] * rest
    above_ghost = (1.0 - ACC_TOP) * mirror + ACC_TOP * (flux[3] / norms[3])[None, :] * moving
    left_value = jnp.where(left_solid > 0.0, left_ghost, left)
    right_value = jnp.where(right_solid > 0.0, right_ghost, right)
    below_value = jnp.where(below_solid > 0.0, below_ghost, below)
    above_value = jnp.where(top_wall > 0.0, above_ghost, above)
    change = jnp.maximum(velocity_x, 0.0) * (center - left_value) + jnp.minimum(velocity_x, 0.0) * (
        right_value - center
    )
    change = (
        change
        + jnp.maximum(velocity_y, 0.0) * (center - below_value)
        + jnp.minimum(velocity_y, 0.0) * (above_value - center)
    )
    return (center - step_size * change) * fluid


def fourier_pass(real_part, imag_part, cosine, sine_table, form, forward):

    def apply(table, values):
        return jnp.einsum(form, table, values, precision=HIGHEST)

    if imag_part is None:
        return (apply(cosine, real_part), -apply(sine_table, real_part))
    if forward:
        return (
            apply(cosine, real_part) + apply(sine_table, imag_part),
            apply(cosine, imag_part) - apply(sine_table, real_part),
        )
    return (
        apply(cosine, real_part) - apply(sine_table, imag_part),
        apply(cosine, imag_part) + apply(sine_table, real_part),
    )


def collide(cube, tables, cosine, sine_table, rate):
    count = cube.shape[0]
    scale = 1.0 / (count * count * count)
    real_part, imag_part = fourier_pass(cube, None, cosine, sine_table, FORMS[0], True)
    real_part, imag_part = fourier_pass(real_part, imag_part, cosine, sine_table, FORMS[1], True)
    real_part, imag_part = fourier_pass(real_part, imag_part, cosine, sine_table, FORMS[2], True)

    def inverse(table):
        factor = table[..., None]
        first_real, first_imag = fourier_pass(
            real_part * factor, imag_part * factor, cosine, sine_table, FORMS[0], False
        )
        second_real, second_imag = fourier_pass(
            first_real, first_imag, cosine, sine_table, FORMS[1], False
        )
        last = jnp.einsum(FORMS[2], cosine, second_real, precision=HIGHEST) - jnp.einsum(
            FORMS[2], sine_table, second_imag, precision=HIGHEST
        )
        return last * scale

    gain = inverse(tables[0]) * inverse(tables[1])
    return cube + rate * (gain - cube * inverse(tables[2]))


def local(dist, cell_type, groove_mask):
    count = VN
    height_count = SY
    volume = count * count * count
    local_y, local_xz, total_cells = dist.shape
    masks = cell_masks(cell_type, groove_mask, height_count)
    norms = wall_norms(count)
    step_size = time_step(count)
    rate = step_size / KNUDSEN
    cosine, sine_table = dft_tables(count)
    tables = kernels(count)
    sub_index = lax.axis_index("sub")
    vel_index = lax.axis_index("vel")
    index_y = sub_index * local_y + jnp.arange(local_y, dtype=jnp.int32)
    index_xz = vel_index * local_xz + jnp.arange(local_xz, dtype=jnp.int32)
    block_shape = (local_y, local_xz)
    velocity_y = jnp.broadcast_to(speeds(index_y, count)[:, None], block_shape).reshape(-1)
    velocity_x = jnp.broadcast_to(speeds(index_xz // count, count)[None, :], block_shape).reshape(
        -1
    )
    velocity_z = jnp.broadcast_to(speeds(index_xz % count, count)[None, :], block_shape).reshape(-1)
    rest, moving, weights = wall_tables(velocity_x, velocity_y, velocity_z)
    velocity = (velocity_x[:, None], velocity_y[:, None], rest[:, None], moving[:, None])
    columns_total = total_cells // height_count
    depth = jnp.sum(cell_type.reshape(columns_total, height_count), axis=1)
    bottom_index = jnp.arange(columns_total, dtype=jnp.int32) * height_count + depth
    state = dist
    for iteration in range(STEPS):
        space = lax.all_to_all(
            lax.all_to_all(state, "vel", split_axis=2, concat_axis=1, tiled=True),
            "sub",
            split_axis=2,
            concat_axis=0,
            tiled=True,
        )
        cells = space.shape[2]
        post = collide(
            space.reshape(count, count, count, cells), tables, cosine, sine_table, rate
        ).reshape(volume, cells)
        back = lax.all_to_all(
            lax.all_to_all(
                post.reshape(count, count * count, 1, cells),
                "vel",
                split_axis=1,
                concat_axis=2,
                tiled=True,
            ),
            "sub",
            split_axis=0,
            concat_axis=3,
            tiled=True,
        )
        center = back.reshape(local_y * local_xz, total_cells)
        flux = lax.psum(jnp.dot(weights, center, precision=HIGHEST), ("vel", "sub"))
        shaped = center.reshape(local_y, local_xz, total_cells)
        bottom_rows = jnp.take(shaped, bottom_index, axis=2)
        top_rows = shaped[:, :, height_count - 1 :: height_count]
        outgoing = jnp.where(sub_index == 0, bottom_rows, top_rows)
        incoming = swapped(outgoing, "sub", 0)
        mirror = jnp.repeat(incoming[::-1], height_count, axis=2).reshape(
            local_y * local_xz, total_cells
        )
        result = advance(
            center,
            jnp.roll(center, height_count, 1),
            jnp.roll(center, -height_count, 1),
            jnp.roll(center, 1, 1),
            jnp.roll(center, -1, 1),
            mirror,
            flux,
            masks,
            velocity,
            norms,
            step_size,
        )
        state = result.reshape(local_y, local_xz, total_cells)
    return state


def solution(mesh):
    return jax.shard_map(
        local,
        mesh=mesh,
        in_specs=(P("sub", "vel", "groups"), P("groups"), P("groups")),
        out_specs=P("sub", "vel", "groups"),
        check_vma=False,
    )
```

profile of v0, /device:TPU:1, one launch (start us, length us, event | category | flops | bytes accessed | tf_op | source)
XLA Modules:
  0.0 529.2 jit_solution(7535001363961206787)
XLA Ops:
  3.6 6.4 %all-to-all-start = ((f32[8,1,16384]{2,1,0:T(1,128)}), f32[8,1,16384]{2,1,0:T(1,128)S(1)}, u32[]{:S(2)}, u32[]{:S(2)}) async-start(f32[8,1,16384]{2,1,0:T(1,128)} %reshape.613), calls=%async_computation | async-start | bytes 1048576 | tf_op jit(solution)/shard_map/all_to_all | solution.py:210
  19.5 3.9 all-to-all-done
  27.4 5.8 %all_to_all.132 = f32[8,256,64]{1,0,2:T(8,128)S(1)} all-to-all(f32[8,256,64]{1,0,2:T(8,128)S(1)} %copy.780), channel_id=1, replica_groups=mesh['groups'=2,'vel'=8,'sub'=2] {'sub'}, dimensions={2} | all-to-all | bytes 1048576 | tf_op jit(solution)/shard_map/all_to_all | solution.py:209
  45.2 3.5 subtract_bitcast_fusion.7
  91.4 3.7 fusion.104
  103.9 3.5 fusion.118
  117.1 3.5 add_bitcast_fusion.6
  128.6 3.8 subtract_bitcast_fusion.4
  155.9 8.6 %fusion.5 = f32[16,16,16,32]{3,0,2,1:T(8,128)} fusion(f32[16,16,16,32]{3,0,2,1:T(8,128)S(1)} %bitcast.348, f32[16,16,32,16]{2,3,1,0:T(8,128)S(1)} %fusion.23, f32[16,16,32,16]{2,3,1,0:T(8,128)S(1)} %fusion.25, f32[16,16,32,16]{2,3,1,0:T(8,128)S(1)} %fusion.29, f32[16,16,32,16]{2,3,1,0:T(8,128)S(1)} %fusion.31, f32[16,16,32,16]{2,3,1,0:T(8,128)S(1)} %fusion.34, ...), kind=kLoop, calls=%fused_computation.9 | loop fusion | flops 1441792 | bytes 4194304 | tf_op jit(solution)/shard_map/add | solution.py:178
  167.7 3.9 all-to-all-start.2
  177.5 7.6 %all-to-all-done.2 = f32[8,1,16384]{2,1,0:T(1,128)S(1)} async-done(((f32[8,1,16384]{2,1,0:T(1,128)}), f32[8,1,16384]{2,1,0:T(1,128)S(1)}, u32[]{:S(2)}, u32[]{:S(2)}) %all-to-all-start.2) | async-done | bytes 524320 | tf_op jit(solution)/shard_map/all_to_all | solution.py:221
  192.3 5.5 %all_to_all.133 = f32[2,1,65536]{2,1,0:T(1,128)S(1)} all-to-all(f32[2,1,65536]{2,1,0:T(1,128)S(1)} %reshape.617), channel_id=1, replica_groups=mesh['groups'=2,'vel'=8,'sub'=2] {'sub'}, dimensions={0} | all-to-all | bytes 1048576 | tf_op jit(solution)/shard_map/all_to_all | solution.py:220
  217.9 30.5 %psum.14 = f32[4,512]{1,0:T(4,128)} all-reduce(f32[4,512]{1,0:T(4,128)} %fusion.572), channel_id=1, replica_groups=mesh['groups'=2,'vel'=8,'sub'=2] {'vel','sub'}, use_global_device_ids=true, to_apply=%region_0.1 | all-reduce | flops 2048 | bytes 16384 | tf_op jit(solution)/shard_map/psum | solution.py:234
  254.5 4.1 slice_divide_fusion.5
  275.2 16.8 %all_to_all.134 = f32[8,1,16384]{2,1,0:T(1,128)S(1)} all-to-all(f32[8,1,16384]{2,1,0:T(1,128)S(1)} %reshape.619), channel_id=1, replica_groups=mesh['groups'=2,'vel'=8,'sub'=2] {'vel'}, dimensions={0} | all-to-all | bytes 1048576 | tf_op jit(solution)/shard_map/all_to_all | solution.py:210
  295.6 4.9 all_to_all.135
  312.4 3.7 subtract_bitcast_fusion.3
  371.1 3.6 fusion.54
  384.3 3.7 add_bitcast_fusion.2
  396.0 3.6 subtract_bitcast_fusion
  423.3 8.6 %fusion.2 = f32[16,16,16,32]{3,0,2,1:T(8,128)} fusion(f32[16,16,16,32]{3,0,2,1:T(8,128)S(1)} %bitcast.345, f32[16,16,32,16]{2,3,1,0:T(8,128)S(1)} %fusion.7, f32[16,16,32,16]{2,3,1,0:T(8,128)S(1)} %fusion.9, f32[16,16,32,16]{2,3,1,0:T(8,128)S(1)} %fusion.13, f32[16,16,32,16]{2,3,1,0:T(8,128)S(1)} %fusion.15, f32[16,16,32,16]{2,3,1,0:T(8,128)S(1)} %fusion.18, ...), kind=kLoop, calls=%fused_computation.5 | loop fusion | flops 1441792 | bytes 4194304 | tf_op jit(solution)/shard_map/add | solution.py:178
  434.4 17.0 %all_to_all.136 = f32[8,1,16384]{2,1,0:T(1,128)S(1)} all-to-all(f32[8,1,16384]{2,1,0:T(1,128)S(1)} %reshape.621), channel_id=1, replica_groups=mesh['groups'=2,'vel'=8,'sub'=2] {'vel'}, dimensions={0} | all-to-all | bytes 1048576 | tf_op jit(solution)/shard_map/all_to_all | solution.py:221
  458.4 5.5 %all_to_all.137 = f32[2,1,65536]{2,1,0:T(1,128)S(1)} all-to-all(f32[2,1,65536]{2,1,0:T(1,128)S(1)} %reshape.623), channel_id=1, replica_groups=mesh['groups'=2,'vel'=8,'sub'=2] {'sub'}, dimensions={0} | all-to-all | bytes 1048576 | tf_op jit(solution)/shard_map/all_to_all | solution.py:220
  481.6 29.9 %psum.15 = f32[4,512]{1,0:T(4,128)S(1)} all-reduce(f32[4,512]{1,0:T(4,128)S(1)} %fusion.571), channel_id=1, replica_groups=mesh['groups'=2,'vel'=8,'sub'=2] {'vel','sub'}, use_global_device_ids=true, to_apply=%region_6.8 | all-reduce | flops 2048 | bytes 16384 | tf_op jit(solution)/shard_map/psum | solution.py:234
  (267 shorter events, 336.1 us)
Async XLA Ops:
  1.8 11.1 %copy-start.33 = (s32[32]{0:T(128)S(1)}, s32[32]{0:T(128)}, u32[]{:S(2)}) copy-start(s32[32]{0:T(128)} %param.7) | copy-start | bytes 388
  1.8 11.1 %copy-start.12 = (s32[512]{0:T(512)S(1)}, s32[512]{0:T(512)}, u32[]{:S(2)}) copy-start(s32[512]{0:T(512)} %param.6) | copy-start | bytes 6148
  3.6 19.8 %all-to-all-start = ((f32[8,1,16384]{2,1,0:T(1,128)}), f32[8,1,16384]{2,1,0:T(1,128)S(1)}, u32[]{:S(2)}, u32[]{:S(2)}) async-start(f32[8,1,16384]{2,1,0:T(1,128)} %reshape.613), calls=%async_computation | async-start | bytes 1048576 | tf_op jit(solution)/shard_map/all_to_all | solution.py:210
  10.5 8.9 %copy-start.23 = (f32[8]{0:T(128)}, f32[8]{0:T(128)S(1)}, u32[]{:S(2)}) copy-start(f32[8]{0:T(128)S(1)} %get-tuple-element.71) | copy-start | bytes 100
  17.3 251.8 %copy-start.13 = (f32[512]{0:T(512)}, f32[512]{0:T(512)S(1)}, u32[]{:S(2)}) copy-start(f32[512]{0:T(512)S(1)} %sub.287) | copy-start | bytes 6148
  164.5 9.8 %copy-start.21 = (f32[496]{0:T(512)S(1)}, f32[496]{0:T(512)}, u32[]{:S(2)}) copy-start(f32[496]{0:T(512)} %get-tuple-element.55) | copy-start | bytes 5956
  164.5 9.8 %copy-start.22 = (f32[496]{0:T(512)S(1)}, f32[496]{0:T(512)}, u32[]{:S(2)}) copy-start(f32[496]{0:T(512)} %get-tuple-element.56) | copy-start | bytes 5956
  164.5 9.8 %copy-start.26 = (f32[16]{0:T(128)S(1)}, f32[16]{0:T(128)}, u32[]{:S(2)}) copy-start(f32[16]{0:T(128)} %get-tuple-element.53) | copy-start | bytes 196
  164.5 9.8 %copy-start.27 = (f32[16]{0:T(128)S(1)}, f32[16]{0:T(128)}, u32[]{:S(2)}) copy-start(f32[16]{0:T(128)} %get-tuple-element.54) | copy-start | bytes 196
  164.5 10.5 %copy-start.32 = (s32[32]{0:T(128)S(1)}, s32[32]{0:T(128)}, u32[]{:S(2)}) copy-start(s32[32]{0:T(128)} %get-tuple-element.11) | copy-start | bytes 388
  164.5 12.9 %copy-start.28 = (f32[8]{0:T(128)S(1)}, f32[8]{0:T(128)}, u32[]{:S(2)}) copy-start(f32[8]{0:T(128)} %get-tuple-element.72) | copy-start | bytes 100
  164.5 12.9 %copy-start.29 = (f32[32]{0:T(128)S(1)}, f32[32]{0:T(128)}, u32[]{:S(2)}) copy-start(f32[32]{0:T(128)} %get-tuple-element.63) | copy-start | bytes 388
  164.5 12.9 %copy-start.30 = (f32[32]{0:T(128)S(1)}, f32[32]{0:T(128)}, u32[]{:S(2)}) copy-start(f32[32]{0:T(128)} %get-tuple-element.64) | copy-start | bytes 388
  164.6 12.9 %copy-start.31 = (f32[32]{0:T(128)S(1)}, f32[32]{0:T(128)}, u32[]{:S(2)}) copy-start(f32[32]{0:T(128)} %get-tuple-element.68) | copy-start | bytes 388
  167.7 17.5 %all-to-all-start.2 = ((f32[8,1,16384]{2,1,0:T(1,128)}), f32[8,1,16384]{2,1,0:T(1,128)S(1)}, u32[]{:S(2)}, u32[]{:S(2)}) async-start(f32[8,1,16384]{2,1,0:T(1,128)} %reshape.615), calls=%async_computation.2 | async-start | bytes 1048576 | tf_op jit(solution)/shard_map/all_to_all | solution.py:221
  177.5 91.6 %copy-start.8 = (f32[8,32]{1,0:T(8,128)}, f32[8,32]{1,0:T(8,128)S(1)}, u32[]{:S(2)}) copy-start(f32[8,32]{1,0:T(8,128)S(1)} %get-tuple-element.57) | copy-start | bytes 3076
  177.5 91.6 %copy-start.10 = (f32[8,32]{1,0:T(8,128)}, f32[8,32]{1,0:T(8,128)S(1)}, u32[]{:S(2)}) copy-start(f32[8,32]{1,0:T(8,128)S(1)} %get-tuple-element.58) | copy-start | bytes 3076
  249.8 15.5 %copy-start.7 = (f32[256,496]{0,1:T(8,128)S(1)}, f32[256,496]{0,1:T(8,128)}, u32[]{:S(2)}) copy-start(f32[256,496]{0,1:T(8,128)} %get-tuple-element.33) | copy-start | bytes 1523716
  249.8 16.5 %copy-start.5 = (f32[256,511]{0,1:T(8,128)S(1)}, f32[256,511]{0,1:T(8,128)}, u32[]{:S(2)}) copy-start(f32[256,511]{0,1:T(8,128)} %get-tuple-element.30) | copy-start | bytes 1569796
  250.9 16.4 %copy-start.4 = (f32[256,511]{0,1:T(8,128)S(1)}, f32[256,511]{0,1:T(8,128)}, u32[]{:S(2)}) copy-start(f32[256,511]{0,1:T(8,128)} %get-tuple-element.31) | copy-start | bytes 1569796
  251.9 16.4 %collective-permute-start = (f32[8,32,32]{2,1,0:T(8,128)S(1)}, f32[8,32,32]{2,1,0:T(8,128)S(1)}, u32[]{:S(2)}, u32[]{:S(2)}) collective-permute-start(f32[8,32,32]{2,1,0:T(8,128)S(1)} %bitcast_select_fusion.1), channel_id=1, source_target_pairs={{0,1},{1,0},{2,3},{3,2},{4,5},{5,4},{6,7},{7,6},{8,9},{9,8},{10,11... | collective-permute-start | bytes 98312 | tf_op jit(solution)/shard_map/ppermute | solution.py:22
  479.6 32.0 %copy-start.16 = (f32[1,512]{1,0:T(1,128)S(1)}, f32[1,512]{1,0:T(1,128)}, u32[]{:S(2)}) copy-start(f32[1,512]{1,0:T(1,128)} %stack_reshape.3) | copy-start | bytes 6148
  479.6 36.1 %copy-start.25 = (pred[32]{0:T(512)(128)(4,1)S(1)}, pred[32]{0:T(512)(128)(4,1)}, u32[]{:S(2)}) copy-start(pred[32]{0:T(512)(128)(4,1)} %get-tuple-element.10) | copy-start | bytes 100
  515.7 9.2 %collective-permute-start.1 = (f32[8,32,32]{2,1,0:T(8,128)S(1)}, f32[8,32,32]{2,1,0:T(8,128)S(1)}, u32[]{:S(2)}, u32[]{:S(2)}) collective-permute-start(f32[8,32,32]{2,1,0:T(8,128)S(1)} %bitcast_select_fusion), channel_id=1, source_target_pairs={{0,1},{1,0},{2,3},{3,2},{4,5},{5,4},{6,7},{7,6},{8,9},{9,8},{10,11... | collective-permute-start | bytes 98312 | tf_op jit(solution)/shard_map/ppermute | solution.py:22
  (14 other events, 45.0 us)
where the time goes:
time: 535 us; the launch traced here: 529 us
  matrix products  244 us (46%)
  blocking collectives  116 us (22%)
  local copies, waits for them, and re-layouts  86.8 us (16%)
  other arithmetic  53.3 us (10%)
  starting transfers between devices  15.7 us (3%)
  waiting for transfers between devices  11.5 us (2%)
    dot_general x68, matrix products, apply(): return jnp.einsum(form, table, values, precision=HIGHEST)  212 us
    psum x2, blocking collectives, local(): flux = lax.psum(jnp.dot(weights, center, precision=HIGHEST), ('vel', 'sub'))  60.4 us
    unnamed x83, local copies, waits for them, and re-layouts  20 us
    add x2, other arithmetic, collide(): return cube + rate * (gain - cube * inverse(tables[2]))  17.1 us
    all_to_all x1, blocking collectives, local(): lax.all_to_all(post.reshape(count, count * count, 1, cells), 'vel', split...  17 us
    all_to_all x1, blocking collectives, local(): lax.all_to_all(state, 'vel', split_axis=2, concat_axis=1, tiled=True)  16.8 us
    dot_general x6, matrix products, inverse(): jnp.einsum(FORMS[2], cosine, second_real, precision=HIGHEST)  15.5 us
    dot_general x6, matrix products, inverse(): jnp.einsum(FORMS[2], sine_table, second_imag, precision=HIGHEST)  15 us
  transfers between devices with their start and end apart: 4, of which 2 were waited for; matrix products, arithmetic and copies ran while one was open for 7% of the time, Pallas kernels for 0%

commit v1 on v0

--- a/solution.py
+++ b/solution.py
@@ -14,6 +14,11 @@
 KNUDSEN = 1.0
 HIGHEST = lax.Precision.HIGHEST
 FORMS = ("kj,jxzc->kxzc", "kj,yjzc->ykzc", "kj,yxjc->yxkc")
+
+
+def axis_by_axis(array, inner_axis, outer_axis):
+    partial = lax.psum(array, inner_axis)
+    return lax.psum(partial, outer_axis)
 
 
 def swapped(value, axis, distance):
@@ -231,7 +236,7 @@
             tiled=True,
         )
         center = back.reshape(local_y * local_xz, total_cells)
-        flux = lax.psum(jnp.dot(weights, center, precision=HIGHEST), ("vel", "sub"))
+        flux = axis_by_axis(jnp.dot(weights, center, precision=HIGHEST), "sub", "vel")
         shaped = center.reshape(local_y, local_xz, total_cells)
         bottom_rows = jnp.take(shaped, bottom_index, axis=2)
         top_rows = shaped[:, :, height_count - 1 :: height_count]

time: 535 us -> 516 us (0.964)
  blocking collectives: 116 us -> 94.2 us
    psum x2 -> x4, blocking collectives: 60.4 us -> 38.7 us  [the longest x2 32.8 us: axis_by_axis(): return lax.psum(partial, outer_axis)]
where the time goes in v1:
time: 516 us; the launch traced here: 510 us
  matrix products  244 us (47%)
  blocking collectives  94.2 us (18%)
  local copies, waits for them, and re-layouts  86.7 us (17%)
  other arithmetic  53 us (10%)
  starting transfers between devices  18.4 us (4%)
  waiting for transfers between devices  11.9 us (2%)
    dot_general x68, matrix products, apply(): return jnp.einsum(form, table, values, precision=HIGHEST)  212 us
    psum x2, blocking collectives, axis_by_axis(): return lax.psum(partial, outer_axis)  32.8 us
    unnamed x83, local copies, waits for them, and re-layouts  20 us
    add x2, other arithmetic, collide(): return cube + rate * (gain - cube * inverse(tables[2]))  17.1 us
    all_to_all x1, blocking collectives, local(): lax.all_to_all(post.reshape(count, count * count, 1, cells), 'vel', split...  17 us
    all_to_all x1, blocking collectives, local(): lax.all_to_all(state, 'vel', split_axis=2, concat_axis=1, tiled=True)  16.8 us
    dot_general x6, matrix products, inverse(): jnp.einsum(FORMS[2], cosine, second_real, precision=HIGHEST)  15.5 us
    dot_general x6, matrix products, inverse(): jnp.einsum(FORMS[2], sine_table, second_imag, precision=HIGHEST)  15 us
  transfers between devices with their start and end apart: 4, of which 2 were waited for; matrix products, arithmetic and copies ran while one was open for 7% of the time, Pallas kernels for 0%

profile of v1, /device:TPU:1, one launch (start us, length us, event | category | flops | bytes accessed | tf_op | source)
XLA Modules:
  0.0 510.2 jit_solution(1484047886181224542)
XLA Ops:
  3.6 6.4 %all-to-all-start = ((f32[8,1,16384]{2,1,0:T(1,128)}), f32[8,1,16384]{2,1,0:T(1,128)S(1)}, u32[]{:S(2)}, u32[]{:S(2)}) async-start(f32[8,1,16384]{2,1,0:T(1,128)} %reshape.613), calls=%async_computation | async-start | bytes 1048576 | tf_op jit(solution)/shard_map/all_to_all | solution.py:215
  19.3 4.1 all-to-all-done
  27.6 5.8 %all_to_all.132 = f32[8,256,64]{1,0,2:T(8,128)S(1)} all-to-all(f32[8,256,64]{1,0,2:T(8,128)S(1)} %copy.780), channel_id=1, replica_groups=mesh['groups'=2,'vel'=8,'sub'=2] {'sub'}, dimensions={2} | all-to-all | bytes 1048576 | tf_op jit(solution)/shard_map/all_to_all | solution.py:214
  45.4 3.5 subtract_bitcast_fusion.7
  91.6 3.7 fusion.104
  128.7 3.8 subtract_bitcast_fusion.4
  156.1 8.6 %fusion.5 = f32[16,16,16,32]{3,0,2,1:T(8,128)} fusion(f32[16,16,16,32]{3,0,2,1:T(8,128)S(1)} %bitcast.348, f32[16,16,32,16]{2,3,1,0:T(8,128)S(1)} %fusion.23, f32[16,16,32,16]{2,3,1,0:T(8,128)S(1)} %fusion.25, f32[16,16,32,16]{2,3,1,0:T(8,128)S(1)} %fusion.29, f32[16,16,32,16]{2,3,1,0:T(8,128)S(1)} %fusion.31, f32[16,16,32,16]{2,3,1,0:T(8,128)S(1)} %fusion.34, ...), kind=kLoop, calls=%fused_computation.9 | loop fusion | flops 1441792 | bytes 4194304 | tf_op jit(solution)/shard_map/add | solution.py:183
  167.8 3.9 all-to-all-start.2
  177.5 7.9 %all-to-all-done.2 = f32[8,1,16384]{2,1,0:T(1,128)S(1)} async-done(((f32[8,1,16384]{2,1,0:T(1,128)}), f32[8,1,16384]{2,1,0:T(1,128)S(1)}, u32[]{:S(2)}, u32[]{:S(2)}) %all-to-all-start.2) | async-done | bytes 524320 | tf_op jit(solution)/shard_map/all_to_all | solution.py:226
  192.6 5.5 %all_to_all.133 = f32[2,1,65536]{2,1,0:T(1,128)S(1)} all-to-all(f32[2,1,65536]{2,1,0:T(1,128)S(1)} %reshape.617), channel_id=1, replica_groups=mesh['groups'=2,'vel'=8,'sub'=2] {'sub'}, dimensions={0} | all-to-all | bytes 1048576 | tf_op jit(solution)/shard_map/all_to_all | solution.py:225
  221.4 16.8 %psum.29 = f32[4,512]{1,0:T(4,128)} all-reduce(f32[4,512]{1,0:T(4,128)} %psum.28), channel_id=1, replica_groups=mesh['groups'=2,'vel'=8,'sub'=2] {'vel'}, use_global_device_ids=true, to_apply=%region_1.2 | all-reduce | flops 2048 | bytes 16384 | tf_op jit(solution)/shard_map/psum | solution.py:21
  241.7 3.9 collective-permute-start
  245.6 3.9 slice_divide_fusion.5
  266.1 16.8 %all_to_all.134 = f32[8,1,16384]{2,1,0:T(1,128)S(1)} all-to-all(f32[8,1,16384]{2,1,0:T(1,128)S(1)} %reshape.619), channel_id=1, replica_groups=mesh['groups'=2,'vel'=8,'sub'=2] {'vel'}, dimensions={0} | all-to-all | bytes 1048576 | tf_op jit(solution)/shard_map/all_to_all | solution.py:215
  286.5 4.9 all_to_all.135
  303.4 3.7 subtract_bitcast_fusion.3
  362.0 3.6 fusion.54
  375.2 3.7 add_bitcast_fusion.2
  386.9 3.6 subtract_bitcast_fusion
  414.2 8.6 %fusion.2 = f32[16,16,16,32]{3,0,2,1:T(8,128)} fusion(f32[16,16,16,32]{3,0,2,1:T(8,128)S(1)} %bitcast.345, f32[16,16,32,16]{2,3,1,0:T(8,128)S(1)} %fusion.7, f32[16,16,32,16]{2,3,1,0:T(8,128)S(1)} %fusion.9, f32[16,16,32,16]{2,3,1,0:T(8,128)S(1)} %fusion.13, f32[16,16,32,16]{2,3,1,0:T(8,128)S(1)} %fusion.15, f32[16,16,32,16]{2,3,1,0:T(8,128)S(1)} %fusion.18, ...), kind=kLoop, calls=%fused_computation.5 | loop fusion | flops 1441792 | bytes 4194304 | tf_op jit(solution)/shard_map/add | solution.py:183
  425.3 17.0 %all_to_all.136 = f32[8,1,16384]{2,1,0:T(1,128)S(1)} all-to-all(f32[8,1,16384]{2,1,0:T(1,128)S(1)} %reshape.621), channel_id=1, replica_groups=mesh['groups'=2,'vel'=8,'sub'=2] {'vel'}, dimensions={0} | all-to-all | bytes 1048576 | tf_op jit(solution)/shard_map/all_to_all | solution.py:226
  449.5 5.5 %all_to_all.137 = f32[2,1,65536]{2,1,0:T(1,128)S(1)} all-to-all(f32[2,1,65536]{2,1,0:T(1,128)S(1)} %reshape.623), channel_id=1, replica_groups=mesh['groups'=2,'vel'=8,'sub'=2] {'sub'}, dimensions={0} | all-to-all | bytes 1048576 | tf_op jit(solution)/shard_map/all_to_all | solution.py:225
  475.5 16.0 %psum.31 = f32[4,512]{1,0:T(4,128)S(1)} all-reduce(f32[4,512]{1,0:T(4,128)S(1)} %psum.30), channel_id=1, replica_groups=mesh['groups'=2,'vel'=8,'sub'=2] {'vel'}, use_global_device_ids=true, to_apply=%region_8.10 | all-reduce | flops 2048 | bytes 16384 | tf_op jit(solution)/shard_map/psum | solution.py:21
  495.4 4.2 collective-permute-start.1
  (269 shorter events, 343.5 us)
Async XLA Ops:
  1.8 11.0 %copy-start.33 = (s32[32]{0:T(128)S(1)}, s32[32]{0:T(128)}, u32[]{:S(2)}) copy-start(s32[32]{0:T(128)} %param.7) | copy-start | bytes 388
  1.8 11.0 %copy-start.12 = (s32[512]{0:T(512)S(1)}, s32[512]{0:T(512)}, u32[]{:S(2)}) copy-start(s32[512]{0:T(512)} %param.6) | copy-start | bytes 6148
  3.6 19.8 %all-to-all-start = ((f32[8,1,16384]{2,1,0:T(1,128)}), f32[8,1,16384]{2,1,0:T(1,128)S(1)}, u32[]{:S(2)}, u32[]{:S(2)}) async-start(f32[8,1,16384]{2,1,0:T(1,128)} %reshape.613), calls=%async_computation | async-start | bytes 1048576 | tf_op jit(solution)/shard_map/all_to_all | solution.py:215
  17.1 242.9 %copy-start.13 = (f32[512]{0:T(512)}, f32[512]{0:T(512)S(1)}, u32[]{:S(2)}) copy-start(f32[512]{0:T(512)S(1)} %sub.287) | copy-start | bytes 6148
  164.7 9.7 %copy-start.21 = (f32[496]{0:T(512)S(1)}, f32[496]{0:T(512)}, u32[]{:S(2)}) copy-start(f32[496]{0:T(512)} %get-tuple-element.55) | copy-start | bytes 5956
  164.7 9.7 %copy-start.22 = (f32[496]{0:T(512)S(1)}, f32[496]{0:T(512)}, u32[]{:S(2)}) copy-start(f32[496]{0:T(512)} %get-tuple-element.56) | copy-start | bytes 5956
  164.7 9.7 %copy-start.26 = (f32[16]{0:T(128)S(1)}, f32[16]{0:T(128)}, u32[]{:S(2)}) copy-start(f32[16]{0:T(128)} %get-tuple-element.53) | copy-start | bytes 196
  164.7 9.7 %copy-start.27 = (f32[16]{0:T(128)S(1)}, f32[16]{0:T(128)}, u32[]{:S(2)}) copy-start(f32[16]{0:T(128)} %get-tuple-element.54) | copy-start | bytes 196
  164.7 10.3 %copy-start.32 = (s32[32]{0:T(128)S(1)}, s32[32]{0:T(128)}, u32[]{:S(2)}) copy-start(s32[32]{0:T(128)} %get-tuple-element.11) | copy-start | bytes 388
  164.7 12.7 %copy-start.28 = (f32[8]{0:T(128)S(1)}, f32[8]{0:T(128)}, u32[]{:S(2)}) copy-start(f32[8]{0:T(128)} %get-tuple-element.72) | copy-start | bytes 100
  164.7 12.7 %copy-start.29 = (f32[32]{0:T(128)S(1)}, f32[32]{0:T(128)}, u32[]{:S(2)}) copy-start(f32[32]{0:T(128)} %get-tuple-element.63) | copy-start | bytes 388
  164.7 12.7 %copy-start.30 = (f32[32]{0:T(128)S(1)}, f32[32]{0:T(128)}, u32[]{:S(2)}) copy-start(f32[32]{0:T(128)} %get-tuple-element.64) | copy-start | bytes 388
  164.7 12.7 %copy-start.31 = (f32[32]{0:T(128)S(1)}, f32[32]{0:T(128)}, u32[]{:S(2)}) copy-start(f32[32]{0:T(128)} %get-tuple-element.68) | copy-start | bytes 388
  167.8 17.5 %all-to-all-start.2 = ((f32[8,1,16384]{2,1,0:T(1,128)}), f32[8,1,16384]{2,1,0:T(1,128)S(1)}, u32[]{:S(2)}, u32[]{:S(2)}) async-start(f32[8,1,16384]{2,1,0:T(1,128)} %reshape.615), calls=%async_computation.2 | async-start | bytes 1048576 | tf_op jit(solution)/shard_map/all_to_all | solution.py:226
  177.5 82.5 %copy-start.8 = (f32[8,32]{1,0:T(8,128)}, f32[8,32]{1,0:T(8,128)S(1)}, u32[]{:S(2)}) copy-start(f32[8,32]{1,0:T(8,128)S(1)} %get-tuple-element.57) | copy-start | bytes 3076
  177.5 82.5 %copy-start.10 = (f32[8,32]{1,0:T(8,128)}, f32[8,32]{1,0:T(8,128)S(1)}, u32[]{:S(2)}) copy-start(f32[8,32]{1,0:T(8,128)S(1)} %get-tuple-element.58) | copy-start | bytes 3076
  239.6 16.6 %copy-start.7 = (f32[256,496]{0,1:T(8,128)S(1)}, f32[256,496]{0,1:T(8,128)}, u32[]{:S(2)}) copy-start(f32[256,496]{0,1:T(8,128)} %get-tuple-element.33) | copy-start | bytes 1523716
  239.6 17.6 %copy-start.5 = (f32[256,511]{0,1:T(8,128)S(1)}, f32[256,511]{0,1:T(8,128)}, u32[]{:S(2)}) copy-start(f32[256,511]{0,1:T(8,128)} %get-tuple-element.30) | copy-start | bytes 1569796
  240.7 17.5 %copy-start.4 = (f32[256,511]{0,1:T(8,128)S(1)}, f32[256,511]{0,1:T(8,128)}, u32[]{:S(2)}) copy-start(f32[256,511]{0,1:T(8,128)} %get-tuple-element.31) | copy-start | bytes 1569796
  241.7 17.5 %collective-permute-start = (f32[8,32,32]{2,1,0:T(8,128)S(1)}, f32[8,32,32]{2,1,0:T(8,128)S(1)}, u32[]{:S(2)}, u32[]{:S(2)}) collective-permute-start(f32[8,32,32]{2,1,0:T(8,128)S(1)} %bitcast_select_fusion.1), channel_id=1, source_target_pairs={{0,1},{1,0},{2,3},{3,2},{4,5},{5,4},{6,7},{7,6},{8,9},{9,8},{10,11... | collective-permute-start | bytes 98312 | tf_op jit(solution)/shard_map/ppermute | solution.py:27
  470.7 20.8 %copy-start.16 = (f32[1,512]{1,0:T(1,128)S(1)}, f32[1,512]{1,0:T(1,128)}, u32[]{:S(2)}) copy-start(f32[1,512]{1,0:T(1,128)} %stack_reshape.3) | copy-start | bytes 6148
  470.7 24.7 %copy-start.25 = (pred[32]{0:T(512)(128)(4,1)S(1)}, pred[32]{0:T(512)(128)(4,1)}, u32[]{:S(2)}) copy-start(pred[32]{0:T(512)(128)(4,1)} %get-tuple-element.10) | copy-start | bytes 100
  495.3 9.5 %copy-start.2 = (f32[256,511]{0,1:T(8,128)S(1)}, f32[256,511]{0,1:T(8,128)}, u32[]{:S(2)}) copy-start(f32[256,511]{0,1:T(8,128)} %get-tuple-element.25) | copy-start | bytes 1569796
  495.4 10.5 %collective-permute-start.1 = (f32[8,32,32]{2,1,0:T(8,128)S(1)}, f32[8,32,32]{2,1,0:T(8,128)S(1)}, u32[]{:S(2)}, u32[]{:S(2)}) collective-permute-start(f32[8,32,32]{2,1,0:T(8,128)S(1)} %bitcast_select_fusion), channel_id=1, source_target_pairs={{0,1},{1,0},{2,3},{3,2},{4,5},{5,4},{6,7},{7,6},{8,9},{9,8},{10,11... | collective-permute-start | bytes 98312 | tf_op jit(solution)/shard_map/ppermute | solution.py:27
  (14 other events, 48.0 us)
